TPU v7x, 32 devices: a whole 2x2x4 slice. The times are simulated.
32 devices in a mesh: gx: 4 (over z), gy: 2 (over y), gz: 4 (over x, core).
Axes of the slice: x: 2, y: 2, z: 4, core: 2. Of those that a mesh axis runs over, the one named last changes fastest.
Arguments:
- density: float32 [64, 16, 1024], P('gx', 'gy', 'gz'), may hold values from 0.05 to 0.95
- voxel_kind: int32 [64, 16, 1024], P('gx', 'gy', 'gz'), may hold values from 0 to 15, as said below
Outputs:
- new_density: float32 [64, 16, 1024], P('gx', 'gy', 'gz')
- velocity: float32 [64, 16, 1024], P('gx', 'gy', 'gz')
- adjoint: float32 [64, 16, 1024], P('gx', 'gy', 'gz')
Inputs may be any that keep to these rules, and one draw needn't show every extreme that they name: `voxel_kind`: 0 to 12 mark design voxels, 13 solid, 14 inlet, 15 outlet.
All inputs are finite; a program needn't handle non-finite values.
Results may differ from a plain program's by a relative error of at most 0.0003.
Values sent between devices are 32-bit elements; how exact they have to be, the bound alone decides.
A program may use at most 128 MiB of HBM per device.

v0:
```python
import jax
import jax.numpy as jnp
from jax import lax
from jax.sharding import PartitionSpec as P

RADIUS = 6
LEVELS = 3
CYCLES = 2
COARSE_SWEEPS = 4
BISECT = 9


penalty_solid = 0.2
penalty_fluid = 0.001
convexity = 0.1
damping = 0.8
step_size = 0.1
move_limit = 0.2
volume_fraction = 0.45
epsilon = 1e-06


def with_halo(cells, sides, width):
    for axis, dim in sides:
        count = lax.axis_size(axis)
        ends = count - 1
        head = lax.slice_in_dim(cells, 0, width, axis=dim)
        tail = lax.slice_in_dim(cells, cells.shape[dim] - width, cells.shape[dim], axis=dim)
        cells = jnp.concatenate(
            [
                lax.ppermute(tail, axis, [(i, (i + 1) % count) for i in range(ends)]),
                cells,
                lax.ppermute(head, axis, [((i + 1) % count, i) for i in range(ends)]),
            ],
            axis=dim,
        )
    return cells


def smooth_axis(padded, axis_dim, length):
    result = None
    for offset in range(-RADIUS, RADIUS + 1):
        tap_term = float(RADIUS + 1 - abs(offset)) * lax.slice_in_dim(
            padded, RADIUS + offset, RADIUS + offset + length, axis=axis_dim
        )
        result = tap_term if result is None else result + tap_term
    return result


def spread(field_values):
    padded = with_halo(field_values, (("gx", 0),), RADIUS)
    field_values = smooth_axis(padded, 0, field_values.shape[0])
    padded = with_halo(field_values, (("gy", 1),), RADIUS)
    field_values = smooth_axis(padded, 1, field_values.shape[1])
    padded = with_halo(field_values, (("gz", 2),), RADIUS)
    return smooth_axis(padded, 2, field_values.shape[2])


def edge_sums(cell_count, first_index, grid_total):
    positions = first_index + jnp.arange(cell_count, dtype=jnp.int32)
    result = jnp.zeros((cell_count,), jnp.float32)
    for offset in range(-RADIUS, RADIUS + 1):
        moved = positions + offset
        inside = (moved >= 0) & (moved < grid_total)
        result = result + jnp.where(inside, float(RADIUS + 1 - abs(offset)), 0.0).astype(
            jnp.float32
        )
    return result


def neighbour_total(padded):
    beside = padded[..., 2:, 1:-1, 1:-1] + padded[..., :-2, 1:-1, 1:-1]
    beside = beside + padded[..., 1:-1, 2:, 1:-1] + padded[..., 1:-1, :-2, 1:-1]
    beside = beside + padded[..., 1:-1, 1:-1, 2:] + padded[..., 1:-1, 1:-1, :-2]
    return beside


def operate(field_values, brinkman_penalty, grid_scale):
    padded = with_halo(field_values, (("gx", 1), ("gy", 2), ("gz", 3)), 1)
    beside = neighbour_total(padded)
    return (6.0 * field_values - beside) * grid_scale + brinkman_penalty * field_values


def relax(field_values, forcing_term, brinkman_penalty, grid_scale, start_blank):
    diagonal = 6.0 * grid_scale + brinkman_penalty
    if start_blank:
        return damping * forcing_term / diagonal
    return (
        field_values
        + damping * (forcing_term - operate(field_values, brinkman_penalty, grid_scale)) / diagonal
    )


def restrict_grid(field_values):
    shape_a, shape_b, shape_c = field_values.shape[-3:]
    blocks = field_values.reshape(
        field_values.shape[:-3] + (shape_a // 2, 2, shape_b // 2, 2, shape_c // 2, 2)
    )
    return jnp.mean(blocks, axis=(-5, -3, -1))


def refine(field_values):
    return jnp.repeat(jnp.repeat(jnp.repeat(field_values, 2, axis=-3), 2, axis=-2), 2, axis=-1)


def multilevel_pass(
    field_values, forcing_term, penalty_pyramid, mesh_depth, start_blank, finest_penalty
):
    grid_scale = 0.25**mesh_depth
    brinkman_penalty = penalty_pyramid[mesh_depth]
    if mesh_depth == LEVELS - 1:
        field_values = relax(None, forcing_term, brinkman_penalty, grid_scale, True)
        for sweep_index in range(COARSE_SWEEPS - 1):
            field_values = relax(field_values, forcing_term, brinkman_penalty, grid_scale, False)
        return field_values
    field_values = relax(field_values, forcing_term, brinkman_penalty, grid_scale, start_blank)
    equation_misfit = forcing_term - operate(field_values, brinkman_penalty, grid_scale)
    coarse_update = multilevel_pass(
        None, restrict_grid(equation_misfit), penalty_pyramid, mesh_depth + 1, True, finest_penalty
    )
    field_values = field_values + refine(coarse_update)
    return relax(field_values, forcing_term, brinkman_penalty, grid_scale, False)


def compute_velocity(forcing_term, penalty_pyramid):
    field_values = None
    for vcycle_counter in range(CYCLES):
        field_values = multilevel_pass(
            field_values, forcing_term, penalty_pyramid, 0, vcycle_counter == 0, None
        )
    return field_values


def global_sums(partials):
    return lax.psum(partials, ("gx", "gy", "gz"))


def body(density, voxel_kind):
    size_x, size_y, size_z = density.shape
    total_x = size_x * lax.axis_size("gx")
    total_y = size_y * lax.axis_size("gy")
    total_z = size_z * lax.axis_size("gz")
    design = voxel_kind < 13
    solid_mask = voxel_kind == 13
    inflow_mask = voxel_kind == 14
    outflow_face = voxel_kind == 15
    sums_x = edge_sums(size_x, lax.axis_index("gx") * size_x, total_x)
    sums_y = edge_sums(size_y, lax.axis_index("gy") * size_y, total_y)
    sums_z = edge_sums(size_z, lax.axis_index("gz") * size_z, total_z)
    normal = sums_x[:, None, None] * sums_y[None, :, None] * sums_z[None, None, :]
    filtered = spread(density) / normal
    interp = penalty_solid + (penalty_fluid - penalty_solid) * filtered * (1.0 + convexity) / (
        filtered + convexity
    )
    brinkman_penalty = jnp.where(
        design, interp, jnp.where(solid_mask, penalty_solid, penalty_fluid)
    )
    penalty_pyramid = [brinkman_penalty]
    for mesh_depth in range(LEVELS - 1):
        penalty_pyramid.append(restrict_grid(penalty_pyramid[-1]))
    inflow_forcing = inflow_mask.astype(jnp.float32)
    outflow_forcing = outflow_face.astype(jnp.float32)
    velocity = compute_velocity(inflow_forcing[None], penalty_pyramid)[0]
    adjoint = compute_velocity(outflow_forcing[None], penalty_pyramid)[0]
    slope = (
        (penalty_fluid - penalty_solid)
        * (1.0 + convexity)
        * convexity
        / ((filtered + convexity) * (filtered + convexity))
    )
    gradient = jnp.where(design, adjoint * velocity * slope, 0.0)
    sensitivity = spread(gradient / normal)
    global_stats = global_sums(
        jnp.stack([jnp.sum(sensitivity * sensitivity), jnp.sum(design.astype(jnp.float32))])
    )
    cell_total = float(total_x * total_y * total_z)
    scaled = sensitivity / jnp.sqrt(global_stats[0] / cell_total + epsilon)
    target = volume_fraction * global_stats[1]
    trial_base = density - step_size * scaled
    lower_bound = jnp.maximum(0.0, density - move_limit)
    upper_bound = jnp.minimum(1.0, density + move_limit)

    def local_volume(candidate):
        return jnp.sum(
            jnp.where(design, jnp.clip(trial_base + candidate, lower_bound, upper_bound), 0.0)
        )

    start_bounds = (jnp.float32(-2.0), jnp.float32(2.0))

    def halve(step_index, bounds):
        low_end, high_end = bounds
        middle = (low_end + high_end) * 0.5
        volume = global_sums(local_volume(middle)[None])[0]
        above_target = volume > target
        return (jnp.where(above_target, low_end, middle), jnp.where(above_target, middle, high_end))

    low_end, high_end = lax.fori_loop(0, BISECT, halve, start_bounds)
    multiplier = (low_end + high_end) * 0.5
    new_density = jnp.where(
        design, jnp.clip(trial_base + multiplier, lower_bound, upper_bound), density
    )
    return (new_density, velocity, adjoint)


def solution(mesh):
    return jax.shard_map(
        body,
        mesh=mesh,
        in_specs=(P("gx", "gy", "gz"), P("gx", "gy", "gz")),
        out_specs=(P("gx", "gy", "gz"), P("gx", "gy", "gz"), P("gx", "gy", "gz")),
        check_vma=False,
    )
```

profile of v0, /device:TPU:0, one launch (start us, length us, event | category | flops | bytes accessed | tf_op | source)
XLA Modules:
  0.0 1169.4 jit_solution(6395994082612991756)
XLA Ops:
  1.5 4.9 collective-permute-start
  14.8 4.6 collective-permute-start.2
  51.8 9.7 reshape.1089
  66.5 9.7 reshape.1088
  81.6 4.8 collective-permute-start.13
  121.3 5.4 collective-permute-done.22
  128.1 4.8 collective-permute-start.25
  154.4 4.6 collective-permute-start.31
  186.8 4.7 collective-permute-start.101
  203.6 9.7 reshape.1093
  240.0 4.8 collective-permute-start.109
  256.0 5.6 collective-permute-done.112
  262.9 4.8 collective-permute-start.115
  284.7 4.8 collective-permute-start.121
  306.8 4.8 collective-permute-start.127
  327.9 4.8 collective-permute-start.43
  334.0 4.6 collective-permute-start.133
  358.5 4.7 collective-permute-start.49
  364.8 6.6 collective-permute-start.137
  417.5 9.7 reshape.1091
  452.7 5.6 collective-permute-start.143
  461.1 4.8 collective-permute-start.67
  482.1 4.8 collective-permute-start.73
  488.2 4.6 collective-permute-start.145
  534.7 4.6 collective-permute-start.85
  540.8 4.7 collective-permute-start.149
  557.6 9.7 reshape.1095
  594.0 4.8 collective-permute-start.157
  610.0 5.6 collective-permute-done.160
  616.9 4.8 collective-permute-start.163
  638.7 4.8 collective-permute-start.169
  652.0 4.8 collective-permute-start.91
  665.6 4.6 collective-permute-start.175
  691.4 4.8 collective-permute-start.181
  710.0 4.8 collective-permute-start.185
  718.7 4.8 collective-permute-start.186
  726.7 4.6 collective-permute-start.188
  742.7 47.0 %psum.14 = f32[2]{0:T(128)S(1)} all-reduce(f32[2]{0:T(128)S(1)} %pad_maximum_fusion.538), channel_id=1, replica_groups=mesh['gx'=4,'gy'=2,'gz'=4] {'gx','gy','gz'}, use_global_device_ids=true, to_apply=%region_12.13 | all-reduce | flops 2 | bytes 16 | tf_op jit(solution)/shard_map/psum | solution.py:135
  791.7 376.6 %while.12 = (s32[]{:T(128)}, f32[]{:T(128)}, f32[]{:T(128)}, f32[16,8,256]{2,1,0:T(8,128)S(1)}, f32[16,8,256]{2,1,0:T(8,128)S(1)}, /*index=5*/f32[16,8,256]{2,1,...) while((s32[]{:T(128)}, f32[]{:T(128)}, f32[]{:T(128)}, ...), condition=%wide.region_16.17_spmd, body=%wide.region_13.16_spmd.sunk | while | flops 163847 | bytes 426160 | solution.py:197
  792.5 40.4 %psum.16 = f32[]{:T(128)} all-reduce(f32[]{:T(128)} %select_reduce_fusion.2), channel_id=1, replica_groups=mesh['gx'=4,'gy'=2,'gz'=4] {'gx','gy','gz'}, use_global_device_ids=true, to_apply=%region_15.15 | all-reduce | flops 1 | bytes 8 | tf_op jit(solution)/shard_map/while/body/eval_jaxpr/psum | solution.py:135
  834.2 40.3 %psum.16 = f32[]{:T(128)} all-reduce(f32[]{:T(128)} %select_reduce_fusion.2), channel_id=1, replica_groups=mesh['gx'=4,'gy'=2,'gz'=4] {'gx','gy','gz'}, use_global_device_ids=true, to_apply=%region_15.15 | all-reduce | flops 1 | bytes 8 | tf_op jit(solution)/shard_map/while/body/eval_jaxpr/psum | solution.py:135
  875.9 40.7 %psum.16 = f32[]{:T(128)} all-reduce(f32[]{:T(128)} %select_reduce_fusion.2), channel_id=1, replica_groups=mesh['gx'=4,'gy'=2,'gz'=4] {'gx','gy','gz'}, use_global_device_ids=true, to_apply=%region_15.15 | all-reduce | flops 1 | bytes 8 | tf_op jit(solution)/shard_map/while/body/eval_jaxpr/psum | solution.py:135
  917.9 40.2 %psum.16 = f32[]{:T(128)} all-reduce(f32[]{:T(128)} %select_reduce_fusion.2), channel_id=1, replica_groups=mesh['gx'=4,'gy'=2,'gz'=4] {'gx','gy','gz'}, use_global_device_ids=true, to_apply=%region_15.15 | all-reduce | flops 1 | bytes 8 | tf_op jit(solution)/shard_map/while/body/eval_jaxpr/psum | solution.py:135
  959.5 40.8 %psum.16 = f32[]{:T(128)} all-reduce(f32[]{:T(128)} %select_reduce_fusion.2), channel_id=1, replica_groups=mesh['gx'=4,'gy'=2,'gz'=4] {'gx','gy','gz'}, use_global_device_ids=true, to_apply=%region_15.15 | all-reduce | flops 1 | bytes 8 | tf_op jit(solution)/shard_map/while/body/eval_jaxpr/psum | solution.py:135
  1001.6 40.2 %psum.16 = f32[]{:T(128)} all-reduce(f32[]{:T(128)} %select_reduce_fusion.2), channel_id=1, replica_groups=mesh['gx'=4,'gy'=2,'gz'=4] {'gx','gy','gz'}, use_global_device_ids=true, to_apply=%region_15.15 | all-reduce | flops 1 | bytes 8 | tf_op jit(solution)/shard_map/while/body/eval_jaxpr/psum | solution.py:135
  1043.2 40.8 %psum.16 = f32[]{:T(128)} all-reduce(f32[]{:T(128)} %select_reduce_fusion.2), channel_id=1, replica_groups=mesh['gx'=4,'gy'=2,'gz'=4] {'gx','gy','gz'}, use_global_device_ids=true, to_apply=%region_15.15 | all-reduce | flops 1 | bytes 8 | tf_op jit(solution)/shard_map/while/body/eval_jaxpr/psum | solution.py:135
  1085.4 40.2 %psum.16 = f32[]{:T(128)} all-reduce(f32[]{:T(128)} %select_reduce_fusion.2), channel_id=1, replica_groups=mesh['gx'=4,'gy'=2,'gz'=4] {'gx','gy','gz'}, use_global_device_ids=true, to_apply=%region_15.15 | all-reduce | flops 1 | bytes 8 | tf_op jit(solution)/shard_map/while/body/eval_jaxpr/psum | solution.py:135
  1126.9 40.8 %psum.16 = f32[]{:T(128)} all-reduce(f32[]{:T(128)} %select_reduce_fusion.2), channel_id=1, replica_groups=mesh['gx'=4,'gy'=2,'gz'=4] {'gx','gy','gz'}, use_global_device_ids=true, to_apply=%region_15.15 | all-reduce | flops 1 | bytes 8 | tf_op jit(solution)/shard_map/while/body/eval_jaxpr/psum | solution.py:135
  (681 shorter events, 540.5 us)
Async XLA Ops:
  47.5 18.1 %collective-permute-start.10 = (f32[1,18,10,1]{3,0,2,1:T(1,128)S(1)}, f32[1,18,10,1]{3,0,2,1:T(1,128)S(1)}, u32[]{:S(2)}, u32[]{:S(2)}) collective-permute-start(f32[1,18,10,1]{3,0,2,1:T(1,128)S(1)} %get-tuple-element.139), channel_id=1, source_target_pairs={{1,0},{2,1},{3,2},{5,4},{6,5},{7,6},{9,8},{10,9},{11,10},{13,12},{... | collective-permute-start | bytes 2168 | tf_op jit(solution)/shard_map/ppermute | solution.py:33
  48.8 16.8 %collective-permute-start.11 = (f32[1,18,10,1]{3,0,2,1:T(1,128)S(1)}, f32[1,18,10,1]{3,0,2,1:T(1,128)S(1)}, u32[]{:S(2)}, u32[]{:S(2)}) collective-permute-start(f32[1,18,10,1]{3,0,2,1:T(1,128)S(1)} %get-tuple-element.140), channel_id=1, source_target_pairs={{0,1},{1,2},{2,3},{4,5},{5,6},{6,7},{8,9},{9,10},{10,11},{12,13},{... | collective-permute-start | bytes 2168 | tf_op jit(solution)/shard_map/ppermute | solution.py:31
  126.8 12.0 %collective-permute-start.24 = (f32[1,1,2,64]{3,1,2,0:T(1,128)S(1)}, f32[1,1,2,64]{3,1,2,0:T(1,128)S(1)}, u32[]{:S(2)}, u32[]{:S(2)}) collective-permute-start(f32[1,1,2,64]{3,1,2,0:T(1,128)S(1)} %get-tuple-element.344), channel_id=1, source_target_pairs={{8,0},{16,8},{24,16},{9,1},{17,9},{25,17},{10,2},{18,10},{26,18},{... | collective-permute-start | bytes 1544 | tf_op jit(solution)/shard_map/ppermute | solution.py:33
  128.1 10.7 collective-permute-start.25
  132.9 11.8 %collective-permute-start.96 = (f32[1,1,8,256]{3,2,1,0:T(8,128)S(1)}, f32[1,1,8,256]{3,2,1,0:T(8,128)S(1)}, u32[]{:S(2)}, u32[]{:S(2)}) collective-permute-start(f32[1,1,8,256]{3,2,1,0:T(8,128)S(1)} %get-tuple-element.212), channel_id=1, source_target_pairs={{8,0},{16,8},{24,16},{9,1},{17,9},{25,17},{10,2},{18,10},{26,18},{... | collective-permute-start | bytes 24584 | tf_op jit(solution)/shard_map/ppermute | solution.py:33
  153.1 11.5 collective-permute-start.30
  159.2 11.4 collective-permute-start.99
  179.4 12.2 %collective-permute-start.36 = (f32[1,1,4,128]{3,2,1,0:T(4,128)S(1)}, f32[1,1,4,128]{3,2,1,0:T(4,128)S(1)}, u32[]{:S(2)}, u32[]{:S(2)}) collective-permute-start(f32[1,1,4,128]{3,2,1,0:T(4,128)S(1)} %get-tuple-element.282), channel_id=1, source_target_pairs={{8,0},{16,8},{24,16},{9,1},{17,9},{25,17},{10,2},{18,10},{26,18},{... | collective-permute-start | bytes 6152 | tf_op jit(solution)/shard_map/ppermute | solution.py:33
  180.7 10.9 collective-permute-start.37
  185.5 11.9 %collective-permute-start.100 = (f32[1,18,10,1]{3,0,2,1:T(1,128)S(1)}, f32[1,18,10,1]{3,0,2,1:T(1,128)S(1)}, u32[]{:S(2)}, u32[]{:S(2)}) collective-permute-start(f32[1,18,10,1]{3,0,2,1:T(1,128)S(1)} %get-tuple-element.159), channel_id=1, source_target_pairs={{1,0},{2,1},{3,2},{5,4},{6,5},{7,6},{9,8},{10,9},{11,10},{13,12},{... | collective-permute-start | bytes 2168 | tf_op jit(solution)/shard_map/ppermute | solution.py:33
  186.8 10.7 collective-permute-start.101
  198.9 18.4 %collective-permute-start.40 = (f32[1,10,6,1]{3,0,2,1:T(1,128)S(1)}, f32[1,10,6,1]{3,0,2,1:T(1,128)S(1)}, u32[]{:S(2)}, u32[]{:S(2)}) collective-permute-start(f32[1,10,6,1]{3,0,2,1:T(1,128)S(1)} %get-tuple-element.229), channel_id=1, source_target_pairs={{1,0},{2,1},{3,2},{5,4},{6,5},{7,6},{9,8},{10,9},{11,10},{13,12},{... | collective-permute-start | bytes 728 | tf_op jit(solution)/shard_map/ppermute | solution.py:33
  200.2 17.1 %collective-permute-start.41 = (f32[1,10,6,1]{3,0,2,1:T(1,128)S(1)}, f32[1,10,6,1]{3,0,2,1:T(1,128)S(1)}, u32[]{:S(2)}, u32[]{:S(2)}) collective-permute-start(f32[1,10,6,1]{3,0,2,1:T(1,128)S(1)} %get-tuple-element.230), channel_id=1, source_target_pairs={{0,1},{1,2},{2,3},{4,5},{5,6},{6,7},{8,9},{9,10},{10,11},{12,13},{... | collective-permute-start | bytes 728 | tf_op jit(solution)/shard_map/ppermute | solution.py:31
  326.6 12.0 %collective-permute-start.42 = (f32[1,1,8,256]{3,2,1,0:T(8,128)S(1)}, f32[1,1,8,256]{3,2,1,0:T(8,128)S(1)}, u32[]{:S(2)}, u32[]{:S(2)}) collective-permute-start(f32[1,1,8,256]{3,2,1,0:T(8,128)S(1)} %get-tuple-element.198), channel_id=1, source_target_pairs={{8,0},{16,8},{24,16},{9,1},{17,9},{25,17},{10,2},{18,10},{26,18},{... | collective-permute-start | bytes 24584 | tf_op jit(solution)/shard_map/ppermute | solution.py:33
  327.9 10.7 collective-permute-start.43
  332.7 11.4 collective-permute-start.132
  338.6 11.7 %collective-permute-start.45 = (f32[1,18,1,256]{3,2,1,0:T(1,128)S(1)}, f32[1,18,1,256]{3,2,1,0:T(1,128)S(1)}, u32[]{:S(2)}, u32[]{:S(2)}) collective-permute-start(f32[1,18,1,256]{3,2,1,0:T(1,128)S(1)} %get-tuple-element.168), channel_id=1, source_target_pairs={{0,4},{1,5},{2,6},{3,7},{8,12},{9,13},{10,14},{11,15},{16,20},{17,... | collective-permute-start | bytes 55304 | tf_op jit(solution)/shard_map/ppermute | solution.py:31
  344.5 10.9 collective-permute-start.135
  357.2 14.2 %collective-permute-start.48 = (f32[1,1,8,256]{3,2,1,0:T(8,128)S(1)}, f32[1,1,8,256]{3,2,1,0:T(8,128)S(1)}, u32[]{:S(2)}, u32[]{:S(2)}) collective-permute-start(f32[1,1,8,256]{3,2,1,0:T(8,128)S(1)} %get-tuple-element.196), channel_id=1, source_target_pairs={{8,0},{16,8},{24,16},{9,1},{17,9},{25,17},{10,2},{18,10},{26,18},{... | collective-permute-start | bytes 24584 | tf_op jit(solution)/shard_map/ppermute | solution.py:33
  358.5 12.9 %collective-permute-start.49 = (f32[1,1,8,256]{3,2,1,0:T(8,128)S(1)}, f32[1,1,8,256]{3,2,1,0:T(8,128)S(1)}, u32[]{:S(2)}, u32[]{:S(2)}) collective-permute-start(f32[1,1,8,256]{3,2,1,0:T(8,128)S(1)} %get-tuple-element.195), channel_id=1, source_target_pairs={{0,8},{8,16},{16,24},{1,9},{9,17},{17,25},{2,10},{10,18},{18,26},{... | collective-permute-start | bytes 24584 | tf_op jit(solution)/shard_map/ppermute | solution.py:31
  363.5 13.9 %collective-permute-start.136 = (f32[1,18,10,1]{3,0,2,1:T(1,128)S(1)}, f32[1,18,10,1]{3,0,2,1:T(1,128)S(1)}, u32[]{:S(2)}, u32[]{:S(2)}) collective-permute-start(f32[1,18,10,1]{3,0,2,1:T(1,128)S(1)} %get-tuple-element.155), channel_id=1, source_target_pairs={{1,0},{2,1},{3,2},{5,4},{6,5},{7,6},{9,8},{10,9},{11,10},{13,12},{... | collective-permute-start | bytes 2168 | tf_op jit(solution)/shard_map/ppermute | solution.py:33
  364.8 12.6 %collective-permute-start.137 = (f32[1,18,10,1]{3,0,2,1:T(1,128)S(1)}, f32[1,18,10,1]{3,0,2,1:T(1,128)S(1)}, u32[]{:S(2)}, u32[]{:S(2)}) collective-permute-start(f32[1,18,10,1]{3,0,2,1:T(1,128)S(1)} %get-tuple-element.156), channel_id=1, source_target_pairs={{0,1},{1,2},{2,3},{4,5},{5,6},{6,7},{8,9},{9,10},{10,11},{12,13},{... | collective-permute-start | bytes 2168 | tf_op jit(solution)/shard_map/ppermute | solution.py:31
  389.0 11.7 %collective-permute-start.54 = (f32[1,1,8,256]{3,2,1,0:T(8,128)S(1)}, f32[1,1,8,256]{3,2,1,0:T(8,128)S(1)}, u32[]{:S(2)}, u32[]{:S(2)}) collective-permute-start(f32[1,1,8,256]{3,2,1,0:T(8,128)S(1)} %get-tuple-element.194), channel_id=1, source_target_pairs={{8,0},{16,8},{24,16},{9,1},{17,9},{25,17},{10,2},{18,10},{26,18},{... | collective-permute-start | bytes 24584 | tf_op jit(solution)/shard_map/ppermute | solution.py:33
  413.5 23.6 %collective-permute-start.141 = (f32[1,18,1,256]{3,2,1,0:T(1,128)S(1)}, f32[1,18,1,256]{3,2,1,0:T(1,128)S(1)}, u32[]{:S(2)}, u32[]{:S(2)}) collective-permute-start(f32[1,18,1,256]{3,2,1,0:T(1,128)S(1)} %get-tuple-element.176), channel_id=1, source_target_pairs={{0,4},{1,5},{2,6},{3,7},{8,12},{9,13},{10,14},{11,15},{16,20},{17,... | collective-permute-start | bytes 55304 | tf_op jit(solution)/shard_map/ppermute | solution.py:31
  415.3 21.8 %collective-permute-start.140 = (f32[1,18,1,256]{3,2,1,0:T(1,128)S(1)}, f32[1,18,1,256]{3,2,1,0:T(1,128)S(1)}, u32[]{:S(2)}, u32[]{:S(2)}) collective-permute-start(f32[1,18,1,256]{3,2,1,0:T(1,128)S(1)} %get-tuple-element.175), channel_id=1, source_target_pairs={{4,0},{5,1},{6,2},{7,3},{12,8},{13,9},{14,10},{15,11},{20,16},{21,... | collective-permute-start | bytes 55304 | tf_op jit(solution)/shard_map/ppermute | solution.py:33
  445.7 12.6 %collective-permute-start.64 = (f32[1,10,6,1]{3,0,2,1:T(1,128)S(1)}, f32[1,10,6,1]{3,0,2,1:T(1,128)S(1)}, u32[]{:S(2)}, u32[]{:S(2)}) collective-permute-start(f32[1,10,6,1]{3,0,2,1:T(1,128)S(1)} %get-tuple-element.225), channel_id=1, source_target_pairs={{1,0},{2,1},{3,2},{5,4},{6,5},{7,6},{9,8},{10,9},{11,10},{13,12},{... | collective-permute-start | bytes 728 | tf_op jit(solution)/shard_map/ppermute | solution.py:33
  447.0 11.3 collective-permute-start.65
  451.4 14.5 %collective-permute-start.142 = (f32[1,18,10,1]{3,0,2,1:T(1,128)S(1)}, f32[1,18,10,1]{3,0,2,1:T(1,128)S(1)}, u32[]{:S(2)}, u32[]{:S(2)}) collective-permute-start(f32[1,18,10,1]{3,0,2,1:T(1,128)S(1)} %get-tuple-element.151), channel_id=1, source_target_pairs={{1,0},{2,1},{3,2},{5,4},{6,5},{7,6},{9,8},{10,9},{11,10},{13,12},{... | collective-permute-start | bytes 2168 | tf_op jit(solution)/shard_map/ppermute | solution.py:33
  452.7 13.2 %collective-permute-start.143 = (f32[1,18,10,1]{3,0,2,1:T(1,128)S(1)}, f32[1,18,10,1]{3,0,2,1:T(1,128)S(1)}, u32[]{:S(2)}, u32[]{:S(2)}) collective-permute-start(f32[1,18,10,1]{3,0,2,1:T(1,128)S(1)} %get-tuple-element.152), channel_id=1, source_target_pairs={{0,1},{1,2},{2,3},{4,5},{5,6},{6,7},{8,9},{9,10},{10,11},{12,13},{... | collective-permute-start | bytes 2168 | tf_op jit(solution)/shard_map/ppermute | solution.py:31
  480.8 12.0 %collective-permute-start.72 = (f32[1,1,2,64]{3,1,2,0:T(1,128)S(1)}, f32[1,1,2,64]{3,1,2,0:T(1,128)S(1)}, u32[]{:S(2)}, u32[]{:S(2)}) collective-permute-start(f32[1,1,2,64]{3,1,2,0:T(1,128)S(1)} %get-tuple-element.338), channel_id=1, source_target_pairs={{8,0},{16,8},{24,16},{9,1},{17,9},{25,17},{10,2},{18,10},{26,18},{... | collective-permute-start | bytes 1544 | tf_op jit(solution)/shard_map/ppermute | solution.py:33
  482.1 10.7 collective-permute-start.73
  486.9 11.8 %collective-permute-start.144 = (f32[1,1,8,256]{3,2,1,0:T(8,128)S(1)}, f32[1,1,8,256]{3,2,1,0:T(8,128)S(1)}, u32[]{:S(2)}, u32[]{:S(2)}) collective-permute-start(f32[1,1,8,256]{3,2,1,0:T(8,128)S(1)} %get-tuple-element.206), channel_id=1, source_target_pairs={{8,0},{16,8},{24,16},{9,1},{17,9},{25,17},{10,2},{18,10},{26,18},{... | collective-permute-start | bytes 24584 | tf_op jit(solution)/shard_map/ppermute | solution.py:33
  507.1 11.5 collective-permute-start.78
  513.2 11.4 collective-permute-start.147
  533.4 12.2 %collective-permute-start.84 = (f32[1,1,4,128]{3,2,1,0:T(4,128)S(1)}, f32[1,1,4,128]{3,2,1,0:T(4,128)S(1)}, u32[]{:S(2)}, u32[]{:S(2)}) collective-permute-start(f32[1,1,4,128]{3,2,1,0:T(4,128)S(1)} %get-tuple-element.270), channel_id=1, source_target_pairs={{8,0},{16,8},{24,16},{9,1},{17,9},{25,17},{10,2},{18,10},{26,18},{... | collective-permute-start | bytes 6152 | tf_op jit(solution)/shard_map/ppermute | solution.py:33
  534.7 10.9 collective-permute-start.85
  539.5 11.9 %collective-permute-start.148 = (f32[1,18,10,1]{3,0,2,1:T(1,128)S(1)}, f32[1,18,10,1]{3,0,2,1:T(1,128)S(1)}, u32[]{:S(2)}, u32[]{:S(2)}) collective-permute-start(f32[1,18,10,1]{3,0,2,1:T(1,128)S(1)} %get-tuple-element.147), channel_id=1, source_target_pairs={{1,0},{2,1},{3,2},{5,4},{6,5},{7,6},{9,8},{10,9},{11,10},{13,12},{... | collective-permute-start | bytes 2168 | tf_op jit(solution)/shard_map/ppermute | solution.py:33
  540.8 10.7 collective-permute-start.149
  553.0 18.4 %collective-permute-start.88 = (f32[1,10,6,1]{3,0,2,1:T(1,128)S(1)}, f32[1,10,6,1]{3,0,2,1:T(1,128)S(1)}, u32[]{:S(2)}, u32[]{:S(2)}) collective-permute-start(f32[1,10,6,1]{3,0,2,1:T(1,128)S(1)} %get-tuple-element.221), channel_id=1, source_target_pairs={{1,0},{2,1},{3,2},{5,4},{6,5},{7,6},{9,8},{10,9},{11,10},{13,12},{... | collective-permute-start | bytes 728 | tf_op jit(solution)/shard_map/ppermute | solution.py:33
  554.3 17.1 %collective-permute-start.89 = (f32[1,10,6,1]{3,0,2,1:T(1,128)S(1)}, f32[1,10,6,1]{3,0,2,1:T(1,128)S(1)}, u32[]{:S(2)}, u32[]{:S(2)}) collective-permute-start(f32[1,10,6,1]{3,0,2,1:T(1,128)S(1)} %get-tuple-element.222), channel_id=1, source_target_pairs={{0,1},{1,2},{2,3},{4,5},{5,6},{6,7},{8,9},{9,10},{10,11},{12,13},{... | collective-permute-start | bytes 728 | tf_op jit(solution)/shard_map/ppermute | solution.py:31
  644.8 12.0 %collective-permute-start.170 = (f32[1,6,1,64]{3,1,2,0:T(8,128)S(1)}, f32[1,6,1,64]{3,1,2,0:T(8,128)S(1)}, u32[]{:S(2)}, u32[]{:S(2)}) collective-permute-start(f32[1,6,1,64]{3,1,2,0:T(8,128)S(1)} %get-tuple-element.324), channel_id=1, source_target_pairs={{4,0},{5,1},{6,2},{7,3},{12,8},{13,9},{14,10},{15,11},{20,16},{21,... | collective-permute-start | bytes 4616 | tf_op jit(solution)/shard_map/ppermute | solution.py:33
  646.1 10.7 collective-permute-start.171
  650.7 19.5 %collective-permute-start.90 = (f32[1,1,8,256]{3,2,1,0:T(8,128)S(1)}, f32[1,1,8,256]{3,2,1,0:T(8,128)S(1)}, u32[]{:S(2)}, u32[]{:S(2)}) collective-permute-start(f32[1,1,8,256]{3,2,1,0:T(8,128)S(1)} %get-tuple-element.192), channel_id=1, source_target_pairs={{8,0},{16,8},{24,16},{9,1},{17,9},{25,17},{10,2},{18,10},{26,18},{... | collective-permute-start | bytes 24584 | tf_op jit(solution)/shard_map/ppermute | solution.py:33
  652.0 18.2 %collective-permute-start.91 = (f32[1,1,8,256]{3,2,1,0:T(8,128)S(1)}, f32[1,1,8,256]{3,2,1,0:T(8,128)S(1)}, u32[]{:S(2)}, u32[]{:S(2)}) collective-permute-start(f32[1,1,8,256]{3,2,1,0:T(8,128)S(1)} %get-tuple-element.191), channel_id=1, source_target_pairs={{0,8},{8,16},{16,24},{1,9},{9,17},{17,25},{2,10},{10,18},{18,26},{... | collective-permute-start | bytes 24584 | tf_op jit(solution)/shard_map/ppermute | solution.py:31
  683.2 13.1 %collective-permute-start.92 = (f32[1,18,1,256]{3,2,1,0:T(1,128)S(1)}, f32[1,18,1,256]{3,2,1,0:T(1,128)S(1)}, u32[]{:S(2)}, u32[]{:S(2)}) collective-permute-start(f32[1,18,1,256]{3,2,1,0:T(1,128)S(1)} %get-tuple-element.162), channel_id=1, source_target_pairs={{4,0},{5,1},{6,2},{7,3},{12,8},{13,9},{14,10},{15,11},{20,16},{21,... | collective-permute-start | bytes 55304 | tf_op jit(solution)/shard_map/ppermute | solution.py:33
  684.5 11.8 %collective-permute-start.93 = (f32[1,18,1,256]{3,2,1,0:T(1,128)S(1)}, f32[1,18,1,256]{3,2,1,0:T(1,128)S(1)}, u32[]{:S(2)}, u32[]{:S(2)}) collective-permute-start(f32[1,18,1,256]{3,2,1,0:T(1,128)S(1)} %get-tuple-element.161), channel_id=1, source_target_pairs={{0,4},{1,5},{2,6},{3,7},{8,12},{9,13},{10,14},{11,15},{16,20},{17,... | collective-permute-start | bytes 55304 | tf_op jit(solution)/shard_map/ppermute | solution.py:31
  697.6 10.6 collective-permute-start.182
  703.8 11.1 collective-permute-start.94
  (145 other events, 1003.8 us)
where the time goes:
time: 1180 us; the launch traced here: 1170 us
  starting transfers between devices  517 us (44%)
  blocking collectives  411 us (35%)
  waiting for transfers between devices  110 us (9%)
  local copies, waits for them, and re-layouts  66.6 us (6%)
  other arithmetic  52.5 us (4%)
    psum x10, blocking collectives, global_sums(): return lax.psum(partials, ('gx', 'gy', 'gz'))  411 us
    ppermute x96, starting transfers between devices, with_halo(): lax.ppermute(tail, axis, [(i, (i + 1) % count) for i in range(ends)])  392 us
    ppermute x96, starting transfers between devices, with_halo(): lax.ppermute(head, axis, [((i + 1) % count, i) for i in range(ends)])  125 us
    ppermute x96, waiting for transfers between devices, with_halo(): lax.ppermute(head, axis, [((i + 1) % count, i) for i in range(ends)])  59.9 us
    reshape x9, local copies, waits for them, and re-layouts, restrict_grid(): field_values.reshape(field_values.shape[:-3] + (shape_a // 2, 2, shape_b...  52.7 us
    ppermute x96, waiting for transfers between devices, with_halo(): lax.ppermute(tail, axis, [(i, (i + 1) % count) for i in range(ends)])  50.4 us
  transfers between devices with their start and end apart: 192, of which 64 were waited for; matrix products, arithmetic and copies ran while one was open for 6% of the time, Pallas kernels for 0%

commit v1 on v0

v1 whole, which is shorter than its diff:
```python
import functools

import jax
import jax.numpy as jnp
from jax import lax
from jax.experimental import pallas as pl
from jax.experimental.pallas import tpu as pltpu
from jax.sharding import PartitionSpec as P

RADIUS = 6
LEVELS = 3
CYCLES = 2
COARSE_SWEEPS = 4
BISECT = 9

penalty_solid = 0.2
penalty_fluid = 0.001
convexity = 0.1
damping = 0.8
step_size = 0.1
move_limit = 0.2
volume_fraction = 0.45
epsilon = 1e-06

MESH = pl.DeviceIdType.MESH
F32 = jnp.float32
FIRST = 31
SECOND = 15


def iota(shape, dim):
    return lax.broadcasted_iota(jnp.int32, shape, dim)


def turn(values, shift, dim):
    shift = shift % values.shape[dim]
    return values if shift == 0 else pltpu.roll(values, shift, dim)


def restrict_pair(pair, stride):
    dy, dz = pair.ndim - 2, pair.ndim - 1
    low = ((iota(pair.shape, dy) // stride) & 1) == 0
    pair = pair + jnp.where(low, turn(pair, -stride, dy), turn(pair, stride, dy))
    low = ((iota(pair.shape, dz) // stride) & 1) == 0
    pair = pair + jnp.where(low, turn(pair, -stride, dz), turn(pair, stride, dz))
    return pair * 0.125


def edge_weight(position, total):
    low = jnp.maximum(RADIUS - position, 0)
    high = jnp.maximum(RADIUS - (total - 1 - position), 0)
    top = (RADIUS + 1) ** 2
    return (top - ((low * (low + 1)) >> 1) - ((high * (high + 1)) >> 1)).astype(F32)


def box(values, count):
    two = values[:-1] + values[1:]
    four = two[:-2] + two[2:]
    return four[:count] + two[4 : 4 + count] + values[6 : 6 + count]


def kernel(
    counts, density, kind, new_density, velocity, adjoint,
    field, filtered, normal, weight_y, weight_z,
    fx_lo, fx_hi, fy_lo, fy_hi, fz_out, fz_lo, fz_hi, f_send, f_recv,
    v0a, v0b, s0, diag0, damp0, v1a, v1b, s1, diag1, damp1, v2a, v2b, s2, damp2,
    mx_lo, mx_hi, my_out, my_lo, my_hi, mz_out, mz_lo, mz_hi, m_send, m_recv,
    q_part, q_one, q_mid, q_two, a_part, a_one, a_mid, a_two, b_part, b_one, b_mid, b_two,
    r_send, r_recv,
):
    nx, ny, nz = density.shape
    cx, cy, cz = counts
    ix, iy, iz = lax.axis_index("gx"), lax.axis_index("gy"), lax.axis_index("gz")
    group = cy * cz
    place = iy * cz + iz

    def group_peer(step):
        other = lax.rem(place + step, group)
        return {"gy": other // cz, "gz": lax.rem(other, cz)}

    def line_peer(step):
        return {"gx": lax.rem(ix + step, cx)}

    has_up = (ix < cx - 1, iy < cy - 1, iz < cz - 1)
    has_down = (ix > 0, iy > 0, iz > 0)
    names = ("gx", "gy", "gz")
    index = (ix, iy, iz)

    def clear(absent, refs):
        @pl.when(jnp.logical_not(absent))
        def _():
            for ref in refs:
                ref[...] = jnp.zeros(ref.shape, F32)

    clear(has_down[0], (fx_lo, mx_lo))
    clear(has_up[0], (fx_hi, mx_hi))
    clear(has_down[1], (fy_lo, my_lo))
    clear(has_up[1], (fy_hi, my_hi))
    clear(has_down[2], (fz_lo, mz_lo))
    clear(has_up[2], (fz_hi, mz_hi))

    barrier = pltpu.get_barrier_semaphore()
    for step in range(1, group):
        pl.semaphore_signal(barrier, inc=1, device_id=group_peer(step), device_id_type=MESH)
    for step in range(1, cx):
        pl.semaphore_signal(barrier, inc=1, device_id=line_peer(step), device_id_type=MESH)

    field[...] = density[...]
    shape = (nx, ny, nz)
    normal[...] = 1.0 / (
        edge_weight(iota(shape, 0) + ix * nx, cx * nx)
        * edge_weight(iota(shape, 1) + iy * ny, cy * ny)
        * edge_weight(iota(shape, 2) + iz * nz, cz * nz)
    )
    rows = nx * ny
    r, c = iota((rows, 3 * rows), 0), iota((rows, 3 * rows), 1)
    block = c // rows
    inner = c - block * rows
    gap = jnp.abs((block - 1) * ny + inner % ny - r % ny)
    weight_y[...] = jnp.where(
        inner // ny == r // ny, jnp.maximum(RADIUS + 1 - gap, 0), 0
    ).astype(F32)
    r, c = iota((nz + 128, nz), 0), iota((nz + 128, nz), 1)
    at = jnp.where(r < 8, nz + r, jnp.where(r < 120, -1000, r - 128))
    weight_z[...] = jnp.maximum(RADIUS + 1 - jnp.abs(at - c), 0).astype(F32)
    for plane in range(nx):
        s0[plane] = jnp.stack(
            [(kind[plane] == 14).astype(F32), (kind[plane] == 15).astype(F32)]
        )

    pl.semaphore_wait(barrier, group - 1 + cx - 1)

    def swap(sends, send_sems, recv_sems):
        copies = []
        for axis, up_src, up_dst, down_src, down_dst in sends:
            for way, src, dst in ((0, up_src, up_dst), (1, down_src, down_dst)):
                def make(axis=axis, way=way, src=src, dst=dst):
                    to = index[axis] + 1 - 2 * way
                    return pltpu.make_async_remote_copy(
                        src_ref=src,
                        dst_ref=dst,
                        send_sem=send_sems.at[2 * axis + way],
                        recv_sem=recv_sems.at[2 * axis + way],
                        device_id={names[axis]: to},
                        device_id_type=MESH,
                    )
                sent = (has_up, has_down)[way][axis]
                got = (has_down, has_up)[way][axis]
                copies.append((make, sent, got))

        for make, sent, got in copies:
            @pl.when(sent)
            def _(make=make):
                make().start()

        for make, sent, got in copies:
            @pl.when(got)
            def _(make=make):
                make().wait_recv()

        for make, sent, got in copies:
            @pl.when(sent)
            def _(make=make):
                make().wait_send()

    def pack_z(source, planes, out):
        tail = head = None
        for plane in range(planes):
            full = source[plane]
            dim = full.ndim - 1
            last = turn(full[..., nz - 128 :], 8 * plane + 8, dim)
            first = turn(full[..., :128], 8 * plane, dim)
            mine = (iota(last.shape, dim) >> 3) == plane
            tail = last if tail is None else jnp.where(mine, last, tail)
            head = first if head is None else jnp.where(mine, first, head)
        out[0] = tail
        out[1] = head

    def spread():
        swap(
            [(0, field.at[pl.ds(nx - RADIUS, RADIUS)], fx_lo, field.at[pl.ds(0, RADIUS)], fx_hi)],
            f_send, f_recv,
        )
        padded = jnp.concatenate([fx_lo[...], field[...], fx_hi[...]], axis=0)
        field[...] = box(box(padded, nx + RADIUS), nx)
        swap([(1, field, fy_lo, field, fy_hi)], f_send, f_recv)
        padded = jnp.concatenate(
            [ref[...].reshape(rows, nz) for ref in (fy_lo, field, fy_hi)], axis=0
        )
        field[...] = jnp.dot(
            weight_y[...], padded, precision=lax.Precision.HIGHEST, preferred_element_type=F32
        ).reshape(nx, ny, nz)
        pack_z(field, nx, fz_out)
        swap([(2, fz_out.at[0], fz_lo, fz_out.at[1], fz_hi)], f_send, f_recv)
        lane = iota((ny, 128), 1)
        parts = []
        for plane in range(nx):
            low = turn(fz_lo[...], 120 - 8 * plane, 1)
            high = turn(fz_hi[...], -8 * plane, 1)
            beside = jnp.where(lane >= 120, low, jnp.where(lane < 8, high, 0.0))
            parts.append(jnp.concatenate([beside, field[plane]], axis=1))
        padded = jnp.concatenate(parts, axis=0)
        field[...] = jnp.dot(
            padded, weight_z[...], precision=lax.Precision.HIGHEST, preferred_element_type=F32
        ).reshape(nx, ny, nz)

    spread()
    smooth = field[...] * normal[...]
    filtered[...] = smooth
    interp = penalty_solid + (penalty_fluid - penalty_solid) * smooth * (1.0 + convexity) / (
        smooth + convexity
    )
    kinds = kind[...]
    penalty = jnp.where(
        kinds < 13, interp, jnp.where(kinds == 13, penalty_solid, penalty_fluid)
    )
    diag0[...] = 6.0 + penalty
    damp0[...] = damping / (6.0 + penalty)
    level1 = []
    for plane in range(nx // 2):
        coarse = restrict_pair(penalty[2 * plane] + penalty[2 * plane + 1], 1)
        level1.append(coarse)
        diag1[plane] = 1.5 + coarse
        damp1[plane] = damping / (1.5 + coarse)
    for plane in range(nx // 4):
        coarse = restrict_pair(level1[2 * plane] + level1[2 * plane + 1], 2)
        damp2[plane] = damping / (0.375 + coarse)

    sub = iota((2, ny, nz), 1)
    lane = iota((2, ny, 128), 2)
    rounds = [0]

    def exchange(source, planes):
        parity = rounds[0] % 2
        rounds[0] += 1
        for plane in range(planes):
            for which in range(2):
                row = 2 * plane + which
                my_out[parity, 0, row : row + 1] = source[plane, which, ny - 1 : ny]
                my_out[parity, 1, row : row + 1] = source[plane, which, 0:1]
        pack_z(source, planes, mz_out.at[parity])
        part = pl.ds(0, 2 * planes)
        swap(
            [
                (0, source.at[planes - 1], mx_lo.at[parity], source.at[0], mx_hi.at[parity]),
                (1, my_out.at[parity, 0, part], my_lo.at[parity, part],
                 my_out.at[parity, 1, part], my_hi.at[parity, part]),
                (2, mz_out.at[parity, 0], mz_lo.at[parity],
                 mz_out.at[parity, 1], mz_hi.at[parity]),
            ],
            m_send.at[parity], m_recv.at[parity],
        )
        return parity

    def both(ref, parity, plane):
        return jnp.stack(
            [
                jnp.broadcast_to(ref[parity, 2 * plane + which : 2 * plane + which + 1], (ny, nz))
                for which in range(2)
            ]
        )

    def beside(source, planes, stride, parity, plane):
        centre = source[plane]
        low = source[plane - 1] if plane else mx_lo[parity]
        high = source[plane + 1] if plane < planes - 1 else mx_hi[parity]
        total = low + high
        low = jnp.where(sub < stride, both(my_lo, parity, plane), turn(centre, stride, 1))
        high = jnp.where(sub >= ny - stride, both(my_hi, parity, plane), turn(centre, -stride, 1))
        total = total + low + high
        low = turn(centre, stride, 2)
        edge = turn(mz_lo[parity], stride - 8 - 8 * plane, 2)
        low = jnp.concatenate(
            [jnp.where(lane < stride, edge, low[..., :128]), low[..., 128:]], axis=2
        )
        high = turn(centre, -stride, 2)
        edge = turn(mz_hi[parity], 128 - stride - 8 * plane, 2)
        high = jnp.concatenate(
            [high[..., : nz - 128], jnp.where(lane >= 128 - stride, edge, high[..., nz - 128 :])],
            axis=2,
        )
        return total + low + high

    def relax(source, target, forcing, damp, planes, stride, scale):
        parity = exchange(source, planes)
        for plane in range(planes):
            total = beside(source, planes, stride, parity, plane)
            target[plane] = (1.0 - damping) * source[plane] + damp[plane][None] * (
                forcing[plane] + scale * total
            )

    def misfit(source, coarse, forcing, diag, planes, stride, scale):
        parity = exchange(source, planes)
        for pair in range(planes // 2):
            total = None
            for plane in (2 * pair, 2 * pair + 1):
                rest = (
                    forcing[plane]
                    - diag[plane][None] * source[plane]
                    + scale * beside(source, planes, stride, parity, plane)
                )
                total = rest if total is None else total + rest
            coarse[pair] = restrict_pair(total, stride)

    now, later = v0a, v0b
    for cycle in range(CYCLES):
        if cycle == 0:
            for plane in range(nx):
                now[plane] = damp0[plane][None] * s0[plane]
        else:
            relax(now, later, s0, damp0, nx, 1, 1.0)
            now, later = later, now
        misfit(now, s1, s0, diag0, nx, 1, 1.0)
        for plane in range(nx // 2):
            v1a[plane] = damp1[plane][None] * s1[plane]
        misfit(v1a, s2, s1, diag1, nx // 2, 2, 0.25)
        for plane in range(nx // 4):
            v2a[plane] = damp2[plane][None] * s2[plane]
        here, there = v2a, v2b
        for sweep in range(COARSE_SWEEPS - 1):
            relax(here, there, s2, damp2, nx // 4, 4, 0.0625)
            here, there = there, here
        for plane in range(nx // 2):
            v1a[plane] = v1a[plane] + here[plane // 2]
        relax(v1a, v1b, s1, damp1, nx // 2, 2, 0.25)
        for plane in range(nx):
            now[plane] = now[plane] + v1b[plane // 2]
        relax(now, later, s0, damp0, nx, 1, 1.0)
        now, later = later, now

    for plane in range(nx):
        flow, dual = now[plane, 0], now[plane, 1]
        velocity[plane] = flow
        adjoint[plane] = dual
        bent = filtered[plane] + convexity
        slope = (penalty_fluid - penalty_solid) * (1.0 + convexity) * convexity / (bent * bent)
        field[plane] = jnp.where(kind[plane] < 13, dual * flow * slope, 0.0) * normal[plane]
    spread()

    sems = [0]

    def total_of(part, one, mid, two):
        def stage(source, target, size, mine, peer):
            copies = []
            for step in range(1, size):
                copy = pltpu.make_async_remote_copy(
                    src_ref=source,
                    dst_ref=target.at[mine],
                    send_sem=r_send.at[sems[0]],
                    recv_sem=r_recv.at[sems[0]],
                    device_id=peer(step),
                    device_id_type=MESH,
                )
                sems[0] += 1
                copy.start()
                copies.append(copy)
            target[mine] = source[...]
            for copy in copies:
                copy.wait_recv()
            total = target[0]
            for other in range(1, size):
                total = total + target[other]
            for copy in copies:
                copy.wait_send()
            return total

        mid[...] = stage(part, one, group, place, group_peer)
        return stage(mid, two, cx, ix, line_peer)

    def fold(values):
        values = jnp.sum(values, axis=0)
        total = values[:, :128]
        for start in range(128, nz, 128):
            total = total + values[:, start : start + 128]
        return total

    def whole(values):
        return jnp.sum(jnp.sum(values, axis=0, keepdims=True), axis=1, keepdims=True)

    design = kind[...] < 13
    sensitivity = field[...]
    q_part[0:8] = fold(sensitivity * sensitivity)
    q_part[8:16] = fold(design.astype(F32))
    stats = total_of(q_part, q_one, q_mid, q_two)
    cells = float(cx * nx * cy * ny * cz * nz)
    spreading = jnp.sqrt(whole(stats[0:8]) / cells + epsilon)
    target = volume_fraction * whole(stats[8:16])
    old = density[...]
    field[...] = old - step_size * (field[...] / spreading[None])
    base = jnp.where(design, field[...], 0.0)
    lower = jnp.where(design, jnp.maximum(0.0, old - move_limit), 0.0)
    upper = jnp.where(design, jnp.minimum(1.0, old + move_limit), 0.0)
    v0a[:, 0] = base
    v0a[:, 1] = lower
    v0b[:, 0] = upper

    def narrow(start, width, trials, part, one, mid, two):
        step = width / (trials + 1)
        part[...] = jnp.zeros(part.shape, F32)
        for trial in range(trials):
            middle = start + (trial + 1) * step
            tried = jnp.minimum(jnp.maximum(v0a[:, 0] + middle[None], v0a[:, 1]), v0b[:, 0])
            part[trial : trial + 1] = jnp.sum(fold(tried), axis=0, keepdims=True)
        volumes = jnp.sum(total_of(part, one, mid, two), axis=1, keepdims=True)
        kept = (iota(volumes.shape, 0) < trials) & jnp.logical_not(volumes > target)
        below = jnp.sum(kept.astype(F32), axis=0, keepdims=True)
        return start + below * step, step

    start, width = jnp.full((1, 1), -2.0, F32), 4.0
    start, width = narrow(start, width, FIRST, a_part, a_one, a_mid, a_two)
    start, width = narrow(start, width, SECOND, b_part, b_one, b_mid, b_two)
    multiplier = start + width * 0.5
    lower = jnp.maximum(0.0, old - move_limit)
    upper = jnp.minimum(1.0, old + move_limit)
    new_density[...] = jnp.where(
        design, jnp.minimum(jnp.maximum(field[...] + multiplier[None], lower), upper), old
    )


def body(counts, density, kind):
    nx, ny, nz = density.shape
    cx, cy, cz = counts
    group = cy * cz
    sends = 3 * (group - 1 + cx - 1)
    vm = lambda *shape: pltpu.VMEM(shape, F32)
    dma = lambda *shape: pltpu.SemaphoreType.DMA(shape)
    cube = (nx, ny, nz)
    half = (nx // 2, ny, nz)
    quarter = (nx // 4, ny, nz)
    pair = lambda planes: vm(planes, 2, ny, nz)

    def sums(count):
        return [vm(count, 128), vm(group, count, 128), vm(count, 128), vm(cx, count, 128)]

    scratch = [
        vm(*cube), vm(*cube), vm(*cube), vm(nx * ny, 3 * nx * ny), vm(nz + 128, nz),
        vm(RADIUS, ny, nz), vm(RADIUS, ny, nz), vm(*cube), vm(*cube),
        vm(2, ny, 128), vm(ny, 128), vm(ny, 128), dma(6), dma(6),
        pair(nx), pair(nx), pair(nx), vm(*cube), vm(*cube),
        pair(nx // 2), pair(nx // 2), pair(nx // 2), vm(*half), vm(*half),
        pair(nx // 4), pair(nx // 4), pair(nx // 4), vm(*quarter),
        vm(2, 2, ny, nz), vm(2, 2, ny, nz),
        vm(2, 2, 2 * nx, nz), vm(2, 2 * nx, nz), vm(2, 2 * nx, nz),
        vm(2, 2, 2, ny, 128), vm(2, 2, ny, 128), vm(2, 2, ny, 128), dma(2, 6), dma(2, 6),
        *sums(16), *sums(FIRST + 1), *sums(SECOND + 1),
        dma(sends), dma(sends),
    ]
    spec = pl.BlockSpec(memory_space=pltpu.VMEM)
    return pl.pallas_call(
        functools.partial(kernel, counts),
        out_shape=[jax.ShapeDtypeStruct(cube, F32)] * 3,
        in_specs=[spec] * 2,
        out_specs=[spec] * 3,
        scratch_shapes=scratch,
        compiler_params=pltpu.CompilerParams(
            collective_id=0, has_side_effects=True, vmem_limit_bytes=40 * 1024 * 1024
        ),
    )(density, kind)


def solution(mesh):
    counts = tuple(mesh.shape[name] for name in ("gx", "gy", "gz"))

    def run(density, kind):
        return tuple(body(counts, density, kind))

    return jax.shard_map(
        run,
        mesh=mesh,
        in_specs=(P("gx", "gy", "gz"), P("gx", "gy", "gz")),
        out_specs=(P("gx", "gy", "gz"), P("gx", "gy", "gz"), P("gx", "gy", "gz")),
        check_vma=False,
    )
```

time: 1180 us -> 100 us (0.08)
  starting transfers between devices: 517 us -> 0 us
  blocking collectives: 411 us -> 0 us
  waiting for transfers between devices: 110 us -> 0 us
  Pallas kernels: 0 us -> 95.5 us
  local copies, waits for them, and re-layouts: 66.6 us -> 3.77 us
  other arithmetic: 52.5 us -> 0 us
    ppermute x192 -> x0, starting transfers between devices: 517 us -> none  [the longest x96 392 us: with_halo(): lax.ppermute(tail, axis, [(i, (i + 1) % count) for i in range(ends)])]
    psum x10 -> x0, blocking collectives: 411 us -> none  [global_sums(): return lax.psum(partials, ('gx', 'gy', 'gz'))]
    ppermute x192 -> x0, waiting for transfers between devices: 110 us -> none  [the longest x96 59.9 us: with_halo(): lax.ppermute(head, axis, [((i + 1) % count, i) for i in range(ends)])]
    pallas_call x0 -> x1, Pallas kernels: none -> 95.5 us  [body(): pl.pallas_call(functools.partial(kernel, counts), out_shape=[jax.ShapeDty...]
    reshape x9 -> x0, local copies, waits for them, and re-layouts: 52.7 us -> none  [restrict_grid(): field_values.reshape(field_values.shape[:-3] + (shape_a // 2, 2, shape_b...]
    reduce_sum x21 -> x0, other arithmetic: 30.2 us -> none  [the longest x10 20.9 us: restrict_grid(): return jnp.mean(blocks, axis=(-5, -3, -1))]
  transfers between devices with their start and end apart: 192 -> 0, of which waited for: 64 -> 0; matrix products, arithmetic and copies ran while one was open for 6% -> 0% of each run, Pallas kernels for 0% -> 0%
where the time goes in v1:
time: 100 us
  Pallas kernels  95.5 us (96%)
  local copies, waits for them, and re-layouts  3.77 us (4%)
    pallas_call x1, Pallas kernels, body(): pl.pallas_call(functools.partial(kernel, counts), out_shape=[jax.ShapeDty...  95.5 us
    unnamed x7, local copies, waits for them, and re-layouts  3.77 us

profile of v1, /device:TPU:0, one launch (start us, length us, event | category | flops | bytes accessed | tf_op | source)
XLA Modules:
  0.0 100.0 jit_solution(11205342063543379497)
XLA Ops:
  0.6 0.0 copy-start
  0.6 0.9 copy-done
  1.5 0.0 copy-start.1
  1.5 0.9 copy-done.1
  2.4 95.5 %shard_map.49 = (f32[16,8,256]{2,1,0:T(8,128)S(1)}, f32[16,8,256]{2,1,0:T(8,128)S(1)}, f32[16,8,256]{2,1,0:T(8,128)S(1)}) custom-call(f32[16,8,256]{2,1,0:T(8,128)S(1)} %copy-done, s32[16,8,256]{2,1,0:T(8,128)S(1)} %copy-done.1), custom_call_target="tpu_custom_call" | custom-call | tf_op jit(solution)/shard_map/pallas_call | solution.py:449
  98.0 0.7 copy.8
  98.7 0.7 copy.9
  99.3 0.7 copy.10
Async XLA Ops:
  0.6 0.9 copy-start
  1.5 0.9 copy-start.1

commit v2 on v1

--- a/solution.py
+++ b/solution.py
@@ -53,32 +53,34 @@
     return (top - ((low * (low + 1)) >> 1) - ((high * (high + 1)) >> 1)).astype(F32)
 
 
-def box(values, count):
-    two = values[:-1] + values[1:]
-    four = two[:-2] + two[2:]
-    return four[:count] + two[4 : 4 + count] + values[6 : 6 + count]
-
-
 def kernel(
     counts, density, kind, new_density, velocity, adjoint,
     field, filtered, normal, weight_y, weight_z,
-    fx_lo, fx_hi, fy_lo, fy_hi, fz_out, fz_lo, fz_hi, f_send, f_recv,
+    padded, fz_out, fz_in, f_send, f_recv,
     v0a, v0b, s0, diag0, damp0, v1a, v1b, s1, diag1, damp1, v2a, v2b, s2, damp2,
     mx_lo, mx_hi, my_out, my_lo, my_hi, mz_out, mz_lo, mz_hi, m_send, m_recv,
-    q_part, q_one, q_mid, q_two, a_part, a_one, a_mid, a_two, b_part, b_one, b_mid, b_two,
-    r_send, r_recv,
+    a_part, b_part, r_out, r_mid, r_one, r_two, r_send, r_recv,
 ):
     nx, ny, nz = density.shape
     cx, cy, cz = counts
     ix, iy, iz = lax.axis_index("gx"), lax.axis_index("gy"), lax.axis_index("gz")
-    group = cy * cz
-    place = iy * cz + iz
-
-    def group_peer(step):
-        other = lax.rem(place + step, group)
-        return {"gy": other // cz, "gz": lax.rem(other, cz)}
-
-    def line_peer(step):
+    lines, one_stage = plan_sums(counts)
+    if one_stage:
+        places = ((ix * cy + iy) * cz + iz,)
+    else:
+        places = (iy * cz + iz, ix)
+    plane_size = cy * cz
+
+    def device_of(flat):
+        rest = lax.rem(flat, plane_size)
+        return {"gx": flat // plane_size, "gy": rest // cz, "gz": lax.rem(rest, cz)}
+
+    def peer_of(stage, step):
+        if one_stage:
+            return device_of(lax.rem(places[0] + step, lines[0]))
+        if stage == 0:
+            other = lax.rem(places[0] + step, lines[0])
+            return {"gy": other // cz, "gz": lax.rem(other, cz)}
         return {"gx": lax.rem(ix + step, cx)}
 
     has_up = (ix < cx - 1, iy < cy - 1, iz < cz - 1)
@@ -92,18 +94,28 @@
             for ref in refs:
                 ref[...] = jnp.zeros(ref.shape, F32)
 
-    clear(has_down[0], (fx_lo, mx_lo))
-    clear(has_up[0], (fx_hi, mx_hi))
-    clear(has_down[1], (fy_lo, my_lo))
-    clear(has_up[1], (fy_hi, my_hi))
-    clear(has_down[2], (fz_lo, mz_lo))
-    clear(has_up[2], (fz_hi, mz_hi))
+    clear(has_down[0], (mx_lo,))
+    clear(has_up[0], (mx_hi,))
+    clear(has_down[1], (my_lo,))
+    clear(has_up[1], (my_hi,))
+    clear(has_down[2], (mz_lo,))
+    clear(has_up[2], (mz_hi,))
+    padded[...] = jnp.zeros(padded.shape, F32)
+    fz_in[...] = jnp.zeros(fz_in.shape, F32)
 
     barrier = pltpu.get_barrier_semaphore()
-    for step in range(1, group):
-        pl.semaphore_signal(barrier, inc=1, device_id=group_peer(step), device_id_type=MESH)
-    for step in range(1, cx):
-        pl.semaphore_signal(barrier, inc=1, device_id=line_peer(step), device_id_type=MESH)
+    devices = cx * cy * cz
+    me = (ix * cy + iy) * cz + iz
+
+    def greet(step):
+        other = device_of(lax.rem(me + step, devices))
+        pl.semaphore_signal(barrier, inc=1, device_id=other, device_id_type=MESH)
+
+    if one_stage:
+        for step in range(1, devices):
+            greet(step)
+    else:
+        lax.fori_loop(1, devices, lambda step, none: (greet(step), none)[1], 0)
 
     field[...] = density[...]
     shape = (nx, ny, nz)
@@ -113,13 +125,14 @@
         * edge_weight(iota(shape, 2) + iz * nz, cz * nz)
     )
     rows = nx * ny
-    r, c = iota((rows, 3 * rows), 0), iota((rows, 3 * rows), 1)
-    block = c // rows
-    inner = c - block * rows
-    gap = jnp.abs((block - 1) * ny + inner % ny - r % ny)
-    weight_y[...] = jnp.where(
-        inner // ny == r // ny, jnp.maximum(RADIUS + 1 - gap, 0), 0
-    ).astype(F32)
+    wide = nx + 2 * RADIUS
+    r, c = iota((rows, 3 * wide * ny), 0), iota((rows, 3 * wide * ny), 1)
+    block = c // (wide * ny)
+    inner = c - block * (wide * ny)
+    gap_y = jnp.abs((block - 1) * ny + inner % ny - r % ny)
+    gap_x = jnp.abs(inner // ny - RADIUS - r // ny)
+    top = RADIUS + 1
+    weight_y[...] = (jnp.maximum(top - gap_y, 0) * jnp.maximum(top - gap_x, 0)).astype(F32)
     r, c = iota((nz + 128, nz), 0), iota((nz + 128, nz), 1)
     at = jnp.where(r < 8, nz + r, jnp.where(r < 120, -1000, r - 128))
     weight_z[...] = jnp.maximum(RADIUS + 1 - jnp.abs(at - c), 0).astype(F32)
@@ -128,7 +141,7 @@
             [(kind[plane] == 14).astype(F32), (kind[plane] == 15).astype(F32)]
         )
 
-    pl.semaphore_wait(barrier, group - 1 + cx - 1)
+    pl.semaphore_wait(barrier, devices - 1)
 
     def swap(sends, send_sems, recv_sems):
         copies = []
@@ -176,32 +189,76 @@
         out[0] = tail
         out[1] = head
 
+    ways = [
+        (dx, dy, dz)
+        for dz in (0, 1, -1) for dx in (0, 1, -1) for dy in (1, -1, 0) if (dx, dy, dz) != (0, 0, 0)
+    ]
+
+    def reachable(way, sign):
+        there = None
+        for axis in range(3):
+            if way[axis]:
+                side = (has_up if way[axis] * sign > 0 else has_down)[axis]
+                there = side if there is None else jnp.logical_and(there, side)
+        return there
+
     def spread():
-        swap(
-            [(0, field.at[pl.ds(nx - RADIUS, RADIUS)], fx_lo, field.at[pl.ds(0, RADIUS)], fx_hi)],
-            f_send, f_recv,
-        )
-        padded = jnp.concatenate([fx_lo[...], field[...], fx_hi[...]], axis=0)
-        field[...] = box(box(padded, nx + RADIUS), nx)
-        swap([(1, field, fy_lo, field, fy_hi)], f_send, f_recv)
-        padded = jnp.concatenate(
-            [ref[...].reshape(rows, nz) for ref in (fy_lo, field, fy_hi)], axis=0
+        padded[1, RADIUS : RADIUS + nx, :, 128:] = field[...]
+        pack_z(field, nx, fz_out)
+
+        def make(number, way):
+            dx, dy, dz = way
+            if dz == 0:
+                start = nx - RADIUS if dx > 0 else 0
+                at = 0 if dx > 0 else RADIUS + nx if dx < 0 else RADIUS
+                size = RADIUS if dx else nx
+                src = field.at[pl.ds(start, size)]
+                dst = padded.at[1 - dy, pl.ds(at, size), :, pl.ds(128, nz)]
+            else:
+                which = 0 if dz > 0 else 1
+                src = fz_out.at[which]
+                dst = fz_in.at[which, 1 - dy, 1 - dx]
+            there = {names[axis]: index[axis] + way[axis] for axis in range(3) if way[axis]}
+            return pltpu.make_async_remote_copy(
+                src_ref=src, dst_ref=dst, send_sem=f_send.at[number],
+                recv_sem=f_recv.at[number], device_id=there, device_id_type=MESH,
+            )
+
+        for number, way in enumerate(ways):
+            @pl.when(reachable(way, 1))
+            def _(number=number, way=way):
+                make(number, way).start()
+
+        for number, way in reversed(list(enumerate(ways))):
+            @pl.when(reachable(way, -1))
+            def _(number=number, way=way):
+                make(number, way).wait_recv()
+
+        for number, way in enumerate(ways):
+            @pl.when(reachable(way, 1))
+            def _(number=number, way=way):
+                make(number, way).wait_send()
+
+        lane = iota((ny, 128), 1)
+        for dy in range(3):
+            for plane in range(wide):
+                if plane < RADIUS:
+                    dx, origin = 0, nx - RADIUS + plane
+                elif plane < RADIUS + nx:
+                    dx, origin = 1, plane - RADIUS
+                else:
+                    dx, origin = 2, plane - RADIUS - nx
+                low = turn(fz_in[0, dy, dx], 120 - 8 * origin, 1)
+                high = turn(fz_in[1, dy, dx], -8 * origin, 1)
+                padded[dy, plane, :, 0:128] = jnp.where(
+                    lane >= 120, low, jnp.where(lane < 8, high, 0.0)
+                )
+        mixed = jnp.dot(
+            weight_y[...], padded[...].reshape(3 * wide * ny, nz + 128),
+            precision=lax.Precision.HIGHEST, preferred_element_type=F32,
         )
         field[...] = jnp.dot(
-            weight_y[...], padded, precision=lax.Precision.HIGHEST, preferred_element_type=F32
-        ).reshape(nx, ny, nz)
-        pack_z(field, nx, fz_out)
-        swap([(2, fz_out.at[0], fz_lo, fz_out.at[1], fz_hi)], f_send, f_recv)
-        lane = iota((ny, 128), 1)
-        parts = []
-        for plane in range(nx):
-            low = turn(fz_lo[...], 120 - 8 * plane, 1)
-            high = turn(fz_hi[...], -8 * plane, 1)
-            beside = jnp.where(lane >= 120, low, jnp.where(lane < 8, high, 0.0))
-            parts.append(jnp.concatenate([beside, field[plane]], axis=1))
-        padded = jnp.concatenate(parts, axis=0)
-        field[...] = jnp.dot(
-            padded, weight_z[...], precision=lax.Precision.HIGHEST, preferred_element_type=F32
+            mixed, weight_z[...], precision=lax.Precision.HIGHEST, preferred_element_type=F32
         ).reshape(nx, ny, nz)
 
     spread()
@@ -339,33 +396,33 @@
 
     sems = [0]
 
-    def total_of(part, one, mid, two):
-        def stage(source, target, size, mine, peer):
+    def total_of(number, row):
+        for stage, size in enumerate(lines):
+            source = (r_out, r_mid)[stage].at[number]
+            target = (r_one, r_two)[stage].at[number]
+            source[...] = row
             copies = []
             for step in range(1, size):
                 copy = pltpu.make_async_remote_copy(
                     src_ref=source,
-                    dst_ref=target.at[mine],
+                    dst_ref=target.at[places[stage]],
                     send_sem=r_send.at[sems[0]],
                     recv_sem=r_recv.at[sems[0]],
-                    device_id=peer(step),
+                    device_id=peer_of(stage, step),
                     device_id_type=MESH,
                 )
                 sems[0] += 1
                 copy.start()
                 copies.append(copy)
-            target[mine] = source[...]
+            target[places[stage]] = row
             for copy in copies:
                 copy.wait_recv()
-            total = target[0]
+            row = target[0]
             for other in range(1, size):
-                total = total + target[other]
+                row = row + target[other]
             for copy in copies:
                 copy.wait_send()
-            return total
-
-        mid[...] = stage(part, one, group, place, group_peer)
-        return stage(mid, two, cx, ix, line_peer)
+        return row
 
     def fold(values):
         values = jnp.sum(values, axis=0)
@@ -379,12 +436,13 @@
 
     design = kind[...] < 13
     sensitivity = field[...]
-    q_part[0:8] = fold(sensitivity * sensitivity)
-    q_part[8:16] = fold(design.astype(F32))
-    stats = total_of(q_part, q_one, q_mid, q_two)
+    spot = iota((1, 128), 1)
+    squares = whole(fold(sensitivity * sensitivity))
+    designs = whole(fold(design.astype(F32)))
+    stats = total_of(0, jnp.where(spot == 0, squares, jnp.where(spot == 1, designs, 0.0)))
     cells = float(cx * nx * cy * ny * cz * nz)
-    spreading = jnp.sqrt(whole(stats[0:8]) / cells + epsilon)
-    target = volume_fraction * whole(stats[8:16])
+    spreading = jnp.sqrt(whole(jnp.where(spot == 0, stats, 0.0)) / cells + epsilon)
+    target = volume_fraction * whole(jnp.where(spot == 1, stats, 0.0))
     old = density[...]
     field[...] = old - step_size * (field[...] / spreading[None])
     base = jnp.where(design, field[...], 0.0)
@@ -394,21 +452,24 @@
     v0a[:, 1] = lower
     v0b[:, 0] = upper
 
-    def narrow(start, width, trials, part, one, mid, two):
+    def narrow(number, start, width, trials, part):
         step = width / (trials + 1)
         part[...] = jnp.zeros(part.shape, F32)
         for trial in range(trials):
             middle = start + (trial + 1) * step
             tried = jnp.minimum(jnp.maximum(v0a[:, 0] + middle[None], v0a[:, 1]), v0b[:, 0])
             part[trial : trial + 1] = jnp.sum(fold(tried), axis=0, keepdims=True)
-        volumes = jnp.sum(total_of(part, one, mid, two), axis=1, keepdims=True)
-        kept = (iota(volumes.shape, 0) < trials) & jnp.logical_not(volumes > target)
-        below = jnp.sum(kept.astype(F32), axis=0, keepdims=True)
+        sums = jnp.sum(part[...], axis=1, keepdims=True)
+        own = iota(part.shape, 0) == iota(part.shape, 1)
+        row = jnp.sum(jnp.where(own, sums, 0.0), axis=0, keepdims=True)
+        volumes = total_of(number, row)
+        kept = (spot < trials) & jnp.logical_not(volumes > target)
+        below = jnp.sum(kept.astype(F32), axis=1, keepdims=True)
         return start + below * step, step
 
     start, width = jnp.full((1, 1), -2.0, F32), 4.0
-    start, width = narrow(start, width, FIRST, a_part, a_one, a_mid, a_two)
-    start, width = narrow(start, width, SECOND, b_part, b_one, b_mid, b_two)
+    start, width = narrow(1, start, width, FIRST, a_part)
+    start, width = narrow(2, start, width, SECOND, b_part)
     multiplier = start + width * 0.5
     lower = jnp.maximum(0.0, old - move_limit)
     upper = jnp.minimum(1.0, old + move_limit)
@@ -417,11 +478,19 @@
     )
 
 
+def plan_sums(counts):
+    cx, cy, cz = counts
+    if cx * cy * cz <= 64:
+        return (cx * cy * cz,), True
+    return (cy * cz, cx), False
+
+
 def body(counts, density, kind):
     nx, ny, nz = density.shape
     cx, cy, cz = counts
-    group = cy * cz
-    sends = 3 * (group - 1 + cx - 1)
+    lines, _ = plan_sums(counts)
+    sends = 3 * (sum(lines) - len(lines))
+    wide = nx + 2 * RADIUS
     vm = lambda *shape: pltpu.VMEM(shape, F32)
     dma = lambda *shape: pltpu.SemaphoreType.DMA(shape)
     cube = (nx, ny, nz)
@@ -429,20 +498,17 @@
     quarter = (nx // 4, ny, nz)
     pair = lambda planes: vm(planes, 2, ny, nz)
 
-    def sums(count):
-        return [vm(count, 128), vm(group, count, 128), vm(count, 128), vm(cx, count, 128)]
-
     scratch = [
-        vm(*cube), vm(*cube), vm(*cube), vm(nx * ny, 3 * nx * ny), vm(nz + 128, nz),
-        vm(RADIUS, ny, nz), vm(RADIUS, ny, nz), vm(*cube), vm(*cube),
-        vm(2, ny, 128), vm(ny, 128), vm(ny, 128), dma(6), dma(6),
+        vm(*cube), vm(*cube), vm(*cube), vm(nx * ny, 3 * wide * ny), vm(nz + 128, nz),
+        vm(3, wide, ny, nz + 128), vm(2, ny, 128), vm(2, 3, 3, ny, 128), dma(26), dma(26),
         pair(nx), pair(nx), pair(nx), vm(*cube), vm(*cube),
         pair(nx // 2), pair(nx // 2), pair(nx // 2), vm(*half), vm(*half),
         pair(nx // 4), pair(nx // 4), pair(nx // 4), vm(*quarter),
         vm(2, 2, ny, nz), vm(2, 2, ny, nz),
         vm(2, 2, 2 * nx, nz), vm(2, 2 * nx, nz), vm(2, 2 * nx, nz),
         vm(2, 2, 2, ny, 128), vm(2, 2, ny, 128), vm(2, 2, ny, 128), dma(2, 6), dma(2, 6),
-        *sums(16), *sums(FIRST + 1), *sums(SECOND + 1),
+        vm(FIRST + 1, 128), vm(SECOND + 1, 128), vm(3, 1, 128), vm(3, 1, 128),
+        vm(3, lines[0], 1, 128), vm(3, lines[-1], 1, 128),
         dma(sends), dma(sends),
     ]
     spec = pl.BlockSpec(memory_space=pltpu.VMEM)

time: 100 us -> 91.4 us (0.914)
  Pallas kernels: 95.5 us -> 86.9 us
    pallas_call x1, Pallas kernels: 95.5 us -> 86.9 us  [body(): pl.pallas_call(functools.partial(kernel, counts), out_shape=[jax.ShapeDty...]
where the time goes in v2:
time: 91.4 us; the launch traced here: 91.3 us
  Pallas kernels  86.9 us (95%)
  local copies, waits for them, and re-layouts  3.77 us (4%)
    pallas_call x1, Pallas kernels, body(): pl.pallas_call(functools.partial(kernel, counts), out_shape=[jax.ShapeDty...  86.9 us
    unnamed x7, local copies, waits for them, and re-layouts  3.77 us

profile of v2, /device:TPU:0, one launch (start us, length us, event | category | flops | bytes accessed | tf_op | source)
XLA Modules:
  0.0 91.3 jit_solution(15313299738468388725)
XLA Ops:
  0.6 0.0 copy-start
  0.6 0.9 copy-done
  1.5 0.0 copy-start.1
  1.5 0.9 copy-done.1
  2.4 86.9 %shard_map.49 = (f32[16,8,256]{2,1,0:T(8,128)S(1)}, f32[16,8,256]{2,1,0:T(8,128)S(1)}, f32[16,8,256]{2,1,0:T(8,128)S(1)}) custom-call(f32[16,8,256]{2,1,0:T(8,128)S(1)} %copy-done, s32[16,8,256]{2,1,0:T(8,128)S(1)} %copy-done.1), custom_call_target="tpu_custom_call" | custom-call | tf_op jit(solution)/shard_map/pallas_call | solution.py:515
  89.3 0.7 copy.8
  90.0 0.7 copy.9
  90.6 0.7 copy.10
Async XLA Ops:
  0.6 0.9 copy-start
  1.5 0.9 copy-start.1

commit v3 on v2

--- a/solution.py
+++ b/solution.py
@@ -58,6 +58,7 @@
     field, filtered, normal, weight_y, weight_z,
     padded, fz_out, fz_in, f_send, f_recv,
     v0a, v0b, s0, diag0, damp0, v1a, v1b, s1, diag1, damp1, v2a, v2b, s2, damp2,
+    c_out, cz_out, c_in, cz_in, c_force, c_damp, c_a, c_b, c_send, c_recv,
     mx_lo, mx_hi, my_out, my_lo, my_hi, mz_out, mz_lo, mz_hi, m_send, m_recv,
     a_part, b_part, r_out, r_mid, r_one, r_two, r_send, r_recv,
 ):
@@ -102,6 +103,8 @@
     clear(has_up[2], (mz_hi,))
     padded[...] = jnp.zeros(padded.shape, F32)
     fz_in[...] = jnp.zeros(fz_in.shape, F32)
+    c_in[...] = jnp.zeros(c_in.shape, F32)
+    cz_in[...] = jnp.zeros(cz_in.shape, F32)
 
     barrier = pltpu.get_barrier_semaphore()
     devices = cx * cy * cz
@@ -283,6 +286,129 @@
         coarse = restrict_pair(level1[2 * plane] + level1[2 * plane + 1], 2)
         damp2[plane] = damping / (0.375 + coarse)
 
+    few = nx // 4
+    deep = cy == 2 and 3 <= few <= 8 and ny == 8
+    reach = COARSE_SWEEPS - 1
+    near = [
+        (dx, dy, dz)
+        for dz in (0, 1, -1) for dx in (0, 1, -1) for dy in (1, 0) if (dx, dy, dz) != (0, 0, 0)
+    ]
+
+    def gather_copy(turn_number, number, way):
+        dx, dy, dz = way
+        if dz == 0:
+            size = reach if dx else few
+            start = few - reach if dx > 0 else 0
+            at = 0 if dx > 0 else reach + few if dx < 0 else reach
+            src = c_out.at[turn_number, pl.ds(start, size)]
+            dst = c_in.at[turn_number, dy, pl.ds(at, size)]
+        else:
+            which = 0 if dz > 0 else 1
+            src = cz_out.at[turn_number, which]
+            dst = cz_in.at[turn_number, which, dy, 1 - dx]
+        there = {}
+        if dx:
+            there["gx"] = ix + dx
+        if dy:
+            there["gy"] = 1 - iy
+        if dz:
+            there["gz"] = iz + dz
+        return pltpu.make_async_remote_copy(
+            src_ref=src, dst_ref=dst, send_sem=c_send.at[turn_number, number],
+            recv_sem=c_recv.at[turn_number, number], device_id=there, device_id_type=MESH,
+        )
+
+    def guarded(way, sign, act):
+        side = reachable((way[0], 0, way[2]), sign)
+        if side is None:
+            act()
+        else:
+            pl.when(side)(act)
+
+    def gather_start(turn_number, first, second):
+        row = iota((ny, nz), 0)
+        other = ((row & 1) ^ (row >> 2)) == 1
+        spot = iota((ny, 128), 1)
+        tail = head = None
+        for plane in range(few):
+            a, b = first(plane), second(plane)
+            a = jnp.where(other, turn(a, 4, 0), a)
+            b = jnp.where(other, turn(b, 4, 0), b)
+            tile = jnp.where(row < 4, a, b)
+            c_out[turn_number, plane] = tile
+            last = turn(tile[:, nz - 128 :], 16 * plane + 16, 1)
+            begin = turn(tile[:, :128], 16 * plane, 1)
+            mine = (spot >> 4) == plane
+            tail = last if tail is None else jnp.where(mine, last, tail)
+            head = begin if head is None else jnp.where(mine, begin, head)
+        cz_out[turn_number, 0] = tail
+        cz_out[turn_number, 1] = head
+        for number, way in enumerate(near):
+            guarded(way, 1, lambda n=number, w=way: gather_copy(turn_number, n, w).start())
+
+    def gather_finish(turn_number, target):
+        for number, way in enumerate(near):
+            guarded(way, -1, lambda n=number, w=way: gather_copy(turn_number, n, w).wait_recv())
+        for number, way in enumerate(near):
+            guarded(way, 1, lambda n=number, w=way: gather_copy(turn_number, n, w).wait_send())
+        spot = iota((ny, 128), 1)
+        mine = ((iota((ny, nz), 0) >> 1) & 1) == iy
+        here = ((iota((ny, 128), 0) >> 1) & 1) == iy
+        for plane in range(few + 2 * reach):
+            if plane < reach:
+                dx, origin = 0, few - reach + plane
+            elif plane < reach + few:
+                dx, origin = 1, plane - reach
+            else:
+                dx, origin = 2, plane - reach - few
+            own = c_out[turn_number, origin] if dx == 1 else c_in[turn_number, 0, plane]
+            low = jnp.where(here, cz_in[turn_number, 0, 0, dx], cz_in[turn_number, 0, 1, dx])
+            high = jnp.where(here, cz_in[turn_number, 1, 0, dx], cz_in[turn_number, 1, 1, dx])
+            low = turn(low, 112 - 16 * origin, 1)
+            high = turn(high, -16 * origin, 1)
+            target[plane, :, 0:128] = jnp.where(
+                spot >= 116, low, jnp.where(spot < 12, high, 0.0)
+            )
+            target[plane, :, 128:] = jnp.where(mine, own, c_in[turn_number, 1, plane])
+
+    def coarse_solve(turn_number):
+        gather_start(turn_number, lambda plane: s2[plane, 0], lambda plane: s2[plane, 1])
+        if turn_number == 1:
+            gather_finish(0, c_damp)
+        gather_finish(turn_number, c_force)
+        tall = few + 2 * reach
+        for plane in range(tall):
+            c_a[plane] = c_damp[plane] * c_force[plane]
+        row = iota((ny, nz + 128), 0) & 3
+        src, dst = c_a, c_b
+        for sweep in range(1, reach + 1):
+            for plane in range(sweep, tall - sweep):
+                centre = src[plane]
+                total = src[plane - 1] + src[plane + 1]
+                total = total + jnp.where(row >= 1, turn(centre, 1, 0), 0.0)
+                total = total + jnp.where(row <= 2, turn(centre, -1, 0), 0.0)
+                total = total + turn(centre, 4, 1) + turn(centre, -4, 1)
+                dst[plane] = (1.0 - damping) * centre + c_damp[plane] * (
+                    c_force[plane] + 0.0625 * total
+                )
+            src, dst = dst, src
+        row = iota((ny, nz), 0)
+        upper_half = (row * 0 + iy) == 1
+        for plane in range(few):
+            tile = src[reach + plane, :, 128:]
+            tile = jnp.where(upper_half, turn(tile, -2, 0), tile)
+            v2a[plane] = jnp.stack([
+                jnp.where(
+                    row < 4,
+                    jnp.broadcast_to(tile[4 * which : 4 * which + 1], (ny, nz)),
+                    jnp.broadcast_to(tile[4 * which + 1 : 4 * which + 2], (ny, nz)),
+                )
+                for which in range(2)
+            ])
+
+    if deep:
+        gather_start(0, lambda plane: damp2[plane], lambda plane: damp2[plane])
+
     sub = iota((2, ny, nz), 1)
     lane = iota((2, ny, 128), 2)
     rounds = [0]
@@ -371,12 +497,15 @@
         for plane in range(nx // 2):
             v1a[plane] = damp1[plane][None] * s1[plane]
         misfit(v1a, s2, s1, diag1, nx // 2, 2, 0.25)
-        for plane in range(nx // 4):
-            v2a[plane] = damp2[plane][None] * s2[plane]
         here, there = v2a, v2b
-        for sweep in range(COARSE_SWEEPS - 1):
-            relax(here, there, s2, damp2, nx // 4, 4, 0.0625)
-            here, there = there, here
+        if deep:
+            coarse_solve(cycle + 1)
+        else:
+            for plane in range(nx // 4):
+                v2a[plane] = damp2[plane][None] * s2[plane]
+            for sweep in range(COARSE_SWEEPS - 1):
+                relax(here, there, s2, damp2, nx // 4, 4, 0.0625)
+                here, there = there, here
         for plane in range(nx // 2):
             v1a[plane] = v1a[plane] + here[plane // 2]
         relax(v1a, v1b, s1, damp1, nx // 2, 2, 0.25)
@@ -491,6 +620,8 @@
     lines, _ = plan_sums(counts)
     sends = 3 * (sum(lines) - len(lines))
     wide = nx + 2 * RADIUS
+    few = nx // 4
+    tall = few + 2 * (COARSE_SWEEPS - 1)
     vm = lambda *shape: pltpu.VMEM(shape, F32)
     dma = lambda *shape: pltpu.SemaphoreType.DMA(shape)
     cube = (nx, ny, nz)
@@ -504,6 +635,9 @@
         pair(nx), pair(nx), pair(nx), vm(*cube), vm(*cube),
         pair(nx // 2), pair(nx // 2), pair(nx // 2), vm(*half), vm(*half),
         pair(nx // 4), pair(nx // 4), pair(nx // 4), vm(*quarter),
+        vm(3, few, ny, nz), vm(3, 2, ny, 128), vm(3, 2, tall, ny, nz), vm(3, 2, 2, 3, ny, 128),
+        vm(tall, ny, nz + 128), vm(tall, ny, nz + 128), vm(tall, ny, nz + 128),
+        vm(tall, ny, nz + 128), dma(3, 17), dma(3, 17),
         vm(2, 2, ny, nz), vm(2, 2, ny, nz),
         vm(2, 2, 2 * nx, nz), vm(2, 2 * nx, nz), vm(2, 2 * nx, nz),
         vm(2, 2, 2, ny, 128), vm(2, 2, ny, 128), vm(2, 2, ny, 128), dma(2, 6), dma(2, 6),

time: 91.4 us -> 84.3 us (0.922)
  Pallas kernels: 86.9 us -> 79.8 us
    pallas_call x1, Pallas kernels: 86.9 us -> 79.8 us  [body(): pl.pallas_call(functools.partial(kernel, counts), out_shape=[jax.ShapeDty...]
where the time goes in v3:
time: 84.3 us; the launch traced here: 84.2 us
  Pallas kernels  79.8 us (95%)
  local copies, waits for them, and re-layouts  3.77 us (4%)
    pallas_call x1, Pallas kernels, body(): pl.pallas_call(functools.partial(kernel, counts), out_shape=[jax.ShapeDty...  79.8 us
    unnamed x7, local copies, waits for them, and re-layouts  3.77 us

profile of v3, /device:TPU:0, one launch (start us, length us, event | category | flops | bytes accessed | tf_op | source)
XLA Modules:
  0.0 84.2 jit_solution(1509066671126092134)
XLA Ops:
  0.6 0.0 copy-start
  0.6 0.9 %copy-done = f32[16,8,256]{2,1,0:T(8,128)S(1)} copy-done((f32[16,8,256]{2,1,0:T(8,128)S(1)}, f32[16,8,256]{2,1,0:T(8,128)}, u32[]{:S(2)}) %copy-start) | copy-done | bytes 131096
  1.5 0.0 copy-start.1
  1.5 0.9 %copy-done.1 = s32[16,8,256]{2,1,0:T(8,128)S(1)} copy-done((s32[16,8,256]{2,1,0:T(8,128)S(1)}, s32[16,8,256]{2,1,0:T(8,128)}, u32[]{:S(2)}) %copy-start.1) | copy-done | bytes 131096
  2.4 79.8 %shard_map.49 = (f32[16,8,256]{2,1,0:T(8,128)S(1)}, f32[16,8,256]{2,1,0:T(8,128)S(1)}, f32[16,8,256]{2,1,0:T(8,128)S(1)}) custom-call(f32[16,8,256]{2,1,0:T(8,128)S(1)} %copy-done, s32[16,8,256]{2,1,0:T(8,128)S(1)} %copy-done.1), custom_call_target="tpu_custom_call" | custom-call | tf_op jit(solution)/shard_map/pallas_call | solution.py:649
  82.2 0.7 copy.8
  82.9 0.7 copy.9
  83.5 0.7 copy.10
Async XLA Ops:
  0.6 0.9 %copy-start = (f32[16,8,256]{2,1,0:T(8,128)S(1)}, f32[16,8,256]{2,1,0:T(8,128)}, u32[]{:S(2)}) copy-start(f32[16,8,256]{2,1,0:T(8,128)} %density.1) | copy-start | bytes 393220
  1.5 0.9 %copy-start.1 = (s32[16,8,256]{2,1,0:T(8,128)S(1)}, s32[16,8,256]{2,1,0:T(8,128)}, u32[]{:S(2)}) copy-start(s32[16,8,256]{2,1,0:T(8,128)} %kind.1) | copy-start | bytes 393220
